TPU v7x, 32 devices: a whole 2x2x4 slice. The times are simulated.
32 devices in a mesh: groups: 2 (over y), tm: 8 (over z, x), space: 2 (over core).
Axes of the slice: x: 2, y: 2, z: 4, core: 2. Of those that a mesh axis runs over, the one named last changes fastest.
Arguments:
- initial: float32 [16, 1024], P(('groups', 'space')), parts along dimension 0, may hold values from -6 to 6
- forcing: float32 [16, 8, 1024], P(('groups', 'tm'), 'space'), parts along dimension 0, may hold values from -1.25 to 1.25
- velocity_x: float32 [16, 1024], P(('groups', 'space')), parts along dimension 0, may hold values from -0.4 to 0.4
- velocity_y: float32 [16, 1024], P(('groups', 'space')), parts along dimension 0, may hold values from -0.4 to 0.4
- cotangent: float32 [16, 8, 1024], P(('groups', 'tm'), 'space'), parts along dimension 0, may hold values from -0.1875 to 0.1875
- w_first: float32 [9, 64, 3], replicated, may hold values from -1.25 to 1.25
- bias_first: float32 [64], replicated, may hold values from -3 to 3
- w_middle: float32 [9, 64, 64], replicated, may hold values from -0.25 to 0.25
- bias_middle: float32 [64], replicated, may hold values from -3 to 3
- w_last: float32 [9, 2, 64], replicated, may hold values from -0.25 to 0.25
- bias_last: float32 [2], replicated, may hold values from -6 to 6
Outputs:
- grad_w_first: float32 [18, 64, 3], P('groups'), parts along dimension 0
- grad_bias_first: float32 [128], P('groups'), parts along dimension 0
- grad_w_middle: float32 [18, 64, 64], P('groups'), parts along dimension 0
- grad_bias_middle: float32 [128], P('groups'), parts along dimension 0
- grad_w_last: float32 [18, 2, 64], P('groups'), parts along dimension 0
- grad_bias_last: float32 [4], P('groups'), parts along dimension 0
There are 2 independent parts, one for each index of `groups`. A program takes and returns all parts, laid end to end along the dimension named above; an argument that names none is the same for every part. Nothing has to cross between parts.
All inputs are finite; a program needn't handle non-finite values.
Results may differ from a plain program's by a relative error of at most 0.0002.
Values sent between devices are 32-bit elements; how exact they have to be, the bound alone decides.
A program may use at most 64 MiB of HBM per device.

v0:
```python
import jax
import jax.numpy as jnp
from jax import lax
from jax.sharding import PartitionSpec as P

FSTEPS = 4


time_step = 0.5
viscosity = 0.2


def extended(shard, sides, width):
    for axis, dim in sides:
        count, length = (lax.axis_size(axis), shard.shape[dim])
        up = [(i, (i + 1) % count) for i in range(count)]
        down = [(j, i) for i, j in up]
        last = lax.slice_in_dim(shard, length - width, length, axis=dim)
        initial = lax.slice_in_dim(shard, 0, width, axis=dim)
        before = lax.ppermute(last, axis, up)
        after = lax.ppermute(initial, axis, down)
        shard = jnp.concatenate([before, shard, after], axis=dim)
    return shard


def entering(value, axis, join, neutral, backward):
    count, mine = (lax.axis_size(axis), lax.axis_index(axis))
    pieces = jax.tree.map(lambda part: lax.all_gather(part, axis), value)
    if backward:
        pieces = jax.tree.map(lambda part: part[::-1], pieces)
        mine = count - 1 - mine
    running = jax.tree.map(
        lambda part, zero: jnp.full_like(part, 0) + jnp.asarray(zero, part.dtype), value, neutral
    )

    def step(position, running):
        longer = join(running, jax.tree.map(lambda part: part[position], pieces))
        return jax.tree.map(lambda new, old: jnp.where(position < mine, new, old), longer, running)

    return lax.fori_loop(0, count - 1, step, running)


def restrict(field):
    shape = field.shape
    blocks = field.reshape(shape[:-2] + (shape[-2] // 4, 4, shape[-1] // 4, 4))
    return blocks.mean(axis=(-3, -1))


def prolong(coarse):
    return jnp.repeat(jnp.repeat(coarse, 4, axis=-2), 4, axis=-1)


def wrap_cols(padded):
    return jnp.concatenate([padded[:, :, -1:], padded, padded[:, :, :1]], axis=2)


def coarse_rim(stack):
    return extended(stack, (("space", 1),), 1)


def rim_rows(stack):
    return extended(stack, (("space", 1),), 1)


def conv_forward(inputs, kernel, offset_bias):
    padded = wrap_cols(coarse_rim(inputs))
    rows_here = inputs.shape[1]
    cols_here = inputs.shape[2]
    output = (
        jnp.zeros((kernel.shape[1], rows_here, cols_here), jnp.float32) + offset_bias[:, None, None]
    )
    for tap_row in range(3):
        for tap_col in range(3):
            window = padded[:, tap_row : tap_row + rows_here, tap_col : tap_col + cols_here]
            output = output + jnp.einsum(
                "oc,crw->orw",
                kernel[3 * tap_row + tap_col],
                window,
                precision=lax.Precision.HIGHEST,
            )
    return (output, padded)


def conv_backward(grad_out, padded, kernel, want_input):
    rows_here = grad_out.shape[1]
    cols_here = grad_out.shape[2]
    kernel_terms = []
    for tap_row in range(3):
        for tap_col in range(3):
            window = padded[:, tap_row : tap_row + rows_here, tap_col : tap_col + cols_here]
            kernel_terms.append(
                jnp.einsum("orw,crw->oc", grad_out, window, precision=lax.Precision.HIGHEST)
            )
    grad_kernel = jnp.stack(kernel_terms)
    grad_bias = jnp.sum(grad_out, axis=(1, 2))
    if not want_input:
        return (grad_kernel, grad_bias, None)
    grad_padded = wrap_cols(coarse_rim(grad_out))
    grad_input = jnp.zeros((kernel.shape[2], rows_here, cols_here), jnp.float32)
    for tap_row in range(3):
        for tap_col in range(3):
            window = grad_padded[
                :, 2 - tap_row : 2 - tap_row + rows_here, 2 - tap_col : 2 - tap_col + cols_here
            ]
            grad_input = grad_input + jnp.einsum(
                "oc,orw->crw",
                kernel[3 * tap_row + tap_col],
                window,
                precision=lax.Precision.HIGHEST,
            )
    return (grad_kernel, grad_bias, grad_input)


def fine_solve(field, forcing, velocity_x, velocity_y):
    for repeat_index in range(FSTEPS):
        padded = rim_rows(field[None])[0]
        upper_row = padded[2:]
        lower_row = padded[:-2]
        east_col = jnp.roll(field, -1, axis=1)
        west_col = jnp.roll(field, 1, axis=1)
        laplace = upper_row + lower_row + east_col + west_col - 4.0 * field
        field = field + time_step * (
            viscosity * laplace
            - velocity_x * (east_col - west_col) * 0.5
            - velocity_y * (upper_row - lower_row) * 0.5
            + forcing
        )
    return field


def fine_adjoint(field, velocity_x, velocity_y):
    for repeat_index in range(FSTEPS):
        padded = rim_rows(jnp.stack([field, velocity_y * field]))
        upper_row = padded[:, 2:]
        lower_row = padded[:, :-2]
        carried = velocity_x * field
        laplace = (
            upper_row[0]
            + lower_row[0]
            + jnp.roll(field, -1, axis=1)
            + jnp.roll(field, 1, axis=1)
            - 4.0 * field
        )
        across = (jnp.roll(carried, -1, axis=1) - jnp.roll(carried, 1, axis=1)) * 0.5
        along = (upper_row[1] - lower_row[1]) * 0.5
        field = field + time_step * (viscosity * laplace + across + along)
    return field


def fold_fine(early, late):
    decay_early, keep_early, term_early = early
    decay_late, keep_late, term_late = late
    coarse_early = restrict(term_early)
    term = (
        term_late
        + prolong(decay_late * coarse_early)
        + keep_late * (term_early - prolong(coarse_early))
    )
    return (decay_late * decay_early, keep_late * keep_early, term)


def forward_states(decay, fine_term, initial):
    unity = jnp.ones_like(decay)
    total_decay, total_keep, total_term = entering(
        (decay, jnp.zeros((), jnp.float32), fine_term),
        "tm",
        fold_fine,
        (unity, jnp.ones((), jnp.float32), jnp.zeros_like(fine_term)),
        False,
    )
    base = restrict(initial)
    start = prolong(total_decay * base) + total_keep * (initial - prolong(base)) + total_term
    return (start, restrict(start))


def backward_adjoint(decay, fine_term):
    unity = jnp.ones_like(decay)
    total_decay, total_keep, total_term = entering(
        (decay, jnp.zeros((), jnp.float32), fine_term),
        "tm",
        fold_fine,
        (unity, jnp.ones((), jnp.float32), jnp.zeros_like(fine_term)),
        True,
    )
    return total_term


def per_device(
    initial,
    forcing,
    velocity_x,
    velocity_y,
    cotangent,
    w_first,
    bias_first,
    w_middle,
    bias_middle,
    w_last,
    bias_last,
):
    forcing = forcing[0]
    cotangent = cotangent[0]
    slices = lax.axis_size("tm")
    rate = 3.0 / slices
    inputs = jnp.stack([restrict(forcing), restrict(velocity_x), restrict(velocity_y)])
    first_pre, padded_one = conv_forward(inputs, w_first, bias_first)
    hidden_one = jnp.tanh(first_pre)
    middle_pre, padded_two = conv_forward(hidden_one, w_middle, bias_middle)
    hidden_two = jnp.tanh(middle_pre)
    output, padded_three = conv_forward(hidden_two, w_last, bias_last)
    gate = jax.nn.sigmoid(output[0])
    decay = jnp.exp(-rate * gate)
    source = output[1] / slices
    start_zero, coarse_zero = forward_states(decay, prolong(source), initial)
    fine_zero = fine_solve(start_zero, forcing, velocity_x, velocity_y)
    start_one, coarse_one = forward_states(decay, fine_zero - prolong(decay * coarse_zero), initial)
    fine_one = fine_solve(start_one, forcing, velocity_x, velocity_y)
    unused, coarse_two = forward_states(decay, fine_one - prolong(decay * coarse_one), initial)
    adjoint_two = cotangent + backward_adjoint(decay, prolong(decay * restrict(cotangent)))
    reduced_two = restrict(adjoint_two)
    pulled_one = fine_adjoint(adjoint_two, velocity_x, velocity_y) - prolong(decay * reduced_two)
    adjoint_one = backward_adjoint(decay, pulled_one)
    reduced_one = restrict(adjoint_one)
    pulled_zero = fine_adjoint(adjoint_one, velocity_x, velocity_y) - prolong(decay * reduced_one)
    adjoint_zero = backward_adjoint(decay, pulled_zero)
    reduced_zero = restrict(adjoint_zero)
    grad_decay = 16.0 * (
        reduced_two * (coarse_two - coarse_one)
        + reduced_one * (coarse_one - coarse_zero)
        + reduced_zero * coarse_zero
    )
    grad_source = 16.0 * reduced_zero
    grad_output = jnp.stack(
        [grad_decay * decay * -rate * gate * (1.0 - gate), grad_source / slices]
    )
    grad_last, grad_bias_last, grad_hidden_two = conv_backward(
        grad_output, padded_three, w_last, True
    )
    grad_middle_pre = grad_hidden_two * (1.0 - hidden_two * hidden_two)
    grad_middle, grad_bias_middle, grad_hidden_one = conv_backward(
        grad_middle_pre, padded_two, w_middle, True
    )
    grad_first_pre = grad_hidden_one * (1.0 - hidden_one * hidden_one)
    grad_first, grad_bias_first, unused_input = conv_backward(
        grad_first_pre, padded_one, w_first, False
    )
    totals = lax.psum(
        (grad_first, grad_bias_first, grad_middle, grad_bias_middle, grad_last, grad_bias_last),
        ("tm", "space"),
    )
    return (totals[0], totals[1], totals[2], totals[3], totals[4], totals[5])


def solution(mesh):
    return jax.shard_map(
        per_device,
        mesh=mesh,
        in_specs=(
            P(("groups", "space"), None),
            P(("groups", "tm"), "space", None),
            P(("groups", "space"), None),
            P(("groups", "space"), None),
            P(("groups", "tm"), "space", None),
            P(),
            P(),
            P(),
            P(),
            P(),
            P(),
        ),
        out_specs=(
            P("groups", None, None),
            P("groups"),
            P("groups", None, None),
            P("groups"),
            P("groups", None, None),
            P("groups"),
        ),
        check_vma=False,
    )
```

profile of v0, /device:TPU:0, one launch (start us, length us, event | category | flops | bytes accessed | tf_op | source)
XLA Modules:
  0.0 481.1 jit_solution(11460300171196439894)
XLA Ops:
  7.2 0.7 reduce_sum.274
  9.4 0.7 collective-permute-done.1
  16.6 0.8 dynamic-update-slice
  17.6 0.8 copy-done.3
  21.7 22.8 %all-reduce = f32[8]{0:T(128)S(1)} all-reduce(f32[8]{0:T(128)S(1)} %dynamic-update-slice), channel_id=1, replica_groups=mesh['groups'=2,'tm'=8,'space'=2] {'tm'}, use_global_device_ids=true, to_apply=%add | all-reduce | flops 8 | bytes 64
  48.7 16.3 %all_gather.25 = f32[8,1,256]{2,1,0:T(1,128)S(1)} all-gather(f32[1,1,256]{2,1,0:T(1,128)S(1)} %get-tuple-element.1027), channel_id=1, replica_groups=mesh['groups'=2,'tm'=8,'space'=2] {'tm'}, dimensions={0}, use_global_device_ids=true | all-gather | bytes 9216 | tf_op jit(solution)/shard_map/all_gather | solution.py:28
  65.2 30.4 %all-gather.1 = f32[8192]{0:T(1024)S(1)} all-gather(f32[1024]{0:T(1024)S(1)} %broadcast_in_dim.259), channel_id=5, replica_groups=mesh['groups'=2,'tm'=8,'space'=2] {'tm'}, dimensions={0}, use_global_device_ids=true | all-gather | bytes 36864 | tf_op jit(solution)/shard_map/all_gather | solution.py:28
  95.6 18.8 %while.97 = (s32[]{:T(128)}, f32[1,256]{1,0:T(1,128)S(1)}, f32[]{:T(128)}, f32[4,1024]{1,0:T(4,128)S(1)}, s32[]{:T(128)}, /*index=5*/f32[8,1,256]{2,1,0:T(1,128)...) while((s32[]{:T(128)}, f32[1,256]{1,0:T(1,128)S(1)}, ...), condition=%wide.region_17.18_spmd.clone, body=%wide.region_14.17_spmd.clone.sunk | while | flops 33798 | bytes 126145 | solution.py:40
  116.0 30.4 %all-gather = f32[8192]{0:T(1024)S(1)} all-gather(f32[1024]{0:T(1024)S(1)} %broadcast_in_dim.256), channel_id=4, replica_groups=mesh['groups'=2,'tm'=8,'space'=2] {'tm'}, dimensions={0}, use_global_device_ids=true | all-gather | bytes 36864 | tf_op jit(solution)/shard_map/all_gather | solution.py:28
  146.5 14.1 %while.96 = (s32[]{:T(128)}, f32[4,1024]{1,0:T(4,128)S(1)}, s32[]{:T(128)}, f32[8,4,1024]{2,1,0:T(4,128)S(1)}, f32[8,1,256]{2,1,0:T(1,128)S(1)}, /*index=5*/f32[8]{0:T(128)S(1)}, s32[]{:T(128)}, s32[]{:T(128)}, f32[]{:T(128)}) while((s32[]{:T(128)}, f32[4,1024]{1,0:T(4,128)S(1)}, s32[]{:T(128)}, f32[8,4,1024]{2,1,0:T(4,128)S(1)}, ...), condition=%wide.region_11.12_spmd.clone, body=%wide.region_8.11_spmd.clone.sunk | while | flops 33028 | bytes 124054 | solution.py:40
  166.8 30.5 %all-gather.6 = f32[8,4,1024]{2,1,0:T(4,128)S(1)} all-gather(f32[1,4,1024]{2,1,0:T(4,128)S(1)} %fusion.298), channel_id=6, replica_groups=mesh['groups'=2,'tm'=8,'space'=2] {'tm'}, dimensions={0}, use_global_device_ids=true | all-gather | bytes 147456 | tf_op jit(solution)/shard_map/all_gather | solution.py:28
  197.3 18.8 %while.98 = (s32[]{:T(128)}, f32[1,256]{1,0:T(1,128)S(1)}, f32[]{:T(128)}, f32[4,1024]{1,0:T(4,128)S(1)}, s32[]{:T(128)}, /*index=5*/f32[8,1,256]{2,1,0:T(1,128)...) while((s32[]{:T(128)}, f32[1,256]{1,0:T(1,128)S(1)}, ...), condition=%wide.region_25.26_spmd.clone, body=%wide.region_22.25_spmd.clone.sunk | while | flops 33798 | bytes 126145 | solution.py:40
  199.3 0.7 fusion.616
  202.0 0.7 fusion.616
  228.6 30.7 %all-gather.8 = f32[8,4,1024]{2,1,0:T(4,128)S(1)} all-gather(f32[1,4,1024]{2,1,0:T(4,128)S(1)} %fusion.203), channel_id=8, replica_groups=mesh['groups'=2,'tm'=8,'space'=2] {'tm'}, dimensions={0}, use_global_device_ids=true | all-gather | bytes 147456 | tf_op jit(solution)/shard_map/all_gather | solution.py:28
  259.3 14.1 %while.100 = (s32[]{:T(128)}, f32[4,1024]{1,0:T(4,128)S(1)}, s32[]{:T(128)}, f32[8,4,1024]{2,1,0:T(4,128)S(1)}, f32[8,1,256]{2,1,0:T(1,128)S(1)}, /*index=5*/f32[8]{0:T(128)S(1)}, s32[]{:T(128)}, s32[]{:T(128)}, f32[]{:T(128)}) while((s32[]{:T(128)}, f32[4,1024]{1,0:T(4,128)S(1)}, s32[]{:T(128)}, f32[8,4,1024]{2,1,0:T(4,128)S(1)}, ...), condition=%wide.region_37.38_spmd.clone, body=%wide.region_34.37_spmd.clone.sunk | while | flops 33028 | bytes 124054 | solution.py:40
  274.4 30.5 %all-gather.7 = f32[8,4,1024]{2,1,0:T(4,128)S(1)} all-gather(f32[1,4,1024]{2,1,0:T(4,128)S(1)} %get-tuple-element.1075), channel_id=7, replica_groups=mesh['groups'=2,'tm'=8,'space'=2] {'tm'}, dimensions={0}, use_global_device_ids=true | all-gather | bytes 147456 | tf_op jit(solution)/shard_map/all_gather | solution.py:28
  304.9 18.8 %while.99 = (s32[]{:T(128)}, f32[1,256]{1,0:T(1,128)S(1)}, f32[]{:T(128)}, f32[4,1024]{1,0:T(4,128)S(1)}, s32[]{:T(128)}, /*index=5*/f32[8,1,256]{2,1,0:T(1,128)...) while((s32[]{:T(128)}, f32[1,256]{1,0:T(1,128)S(1)}, ...), condition=%wide.region_31.32_spmd.clone, body=%wide.region_28.31_spmd.clone.sunk | while | flops 33798 | bytes 126145 | solution.py:40
  330.3 30.5 %all-gather.9 = f32[8,4,1024]{2,1,0:T(4,128)S(1)} all-gather(f32[1,4,1024]{2,1,0:T(4,128)S(1)} %fusion.153), channel_id=9, replica_groups=mesh['groups'=2,'tm'=8,'space'=2] {'tm'}, dimensions={0}, use_global_device_ids=true | all-gather | bytes 147456 | tf_op jit(solution)/shard_map/all_gather | solution.py:28
  360.8 14.1 %while.101 = (s32[]{:T(128)}, f32[4,1024]{1,0:T(4,128)S(1)}, s32[]{:T(128)}, f32[8,4,1024]{2,1,0:T(4,128)S(1)}, f32[8,1,256]{2,1,0:T(1,128)S(1)}, /*index=5*/f32[8]{0:T(128)S(1)}, s32[]{:T(128)}, s32[]{:T(128)}, f32[]{:T(128)}) while((s32[]{:T(128)}, f32[4,1024]{1,0:T(4,128)S(1)}, s32[]{:T(128)}, f32[8,4,1024]{2,1,0:T(4,128)S(1)}, ...), condition=%wide.region_43.44_spmd.clone, body=%wide.region_40.43_spmd.clone.sunk | while | flops 33028 | bytes 124054 | solution.py:40
  382.7 0.7 copy-done.4
  387.8 59.8 %all-reduce.1 = (f32[9,64,3]{1,2,0:T(4,128)}, f32[64]{0:T(128)}, f32[64]{0:T(128)}, f32[9,2,64]{2,1,0:T(2,128)}, f32[2]{0:T(128)}) all-reduce(f32[9,64,3]{1,2,0:T(4,128)S(1)} %fusion.39, f32[64]{0:T(128)S(1)} %get-tuple-element.1216, f32[64]{0:T(128)S(1)} %get-tuple-element.1218, ...), channel_id=1, replica_groups=mesh['groups'=2,'tm'=8,'space'=2] {'tm','space'}, use_global_device_ids=true, to_apply=%region_46.47 | all-reduce | flops 3010 | bytes 24080 | tf_op jit(solution)/shard_map/psum | solution.py:247
  447.6 25.0 %all-reduce.4.cloned.1.call-done = f32[9,64,64]{2,1,0:T(8,128)} async-done(((f32[9,64,64]{2,1,0:T(8,128)}), f32[9,64,64]{2,1,0:T(8,128)}) %all-reduce.4.cloned.1.call-update) | async-done | bytes 147472 | tf_op jit(solution)/shard_map/psum | solution.py:247
  472.6 1.7 copy.263
  (831 shorter events, 135.3 us)
Async XLA Ops:
  7.2 465.4 %all-reduce.4.cloned.1.call-start = ((), (), s32[]{:S(2)}) async-start(), calls=%async_computation | async-start | bytes 589824 | tf_op jit(solution)/shard_map/psum | solution.py:247
  8.8 1.3 collective-permute-start.1
  14.5 2.9 collective-permute-start.3
  14.8 2.6 collective-permute-start.2
  21.1 24.6 %collective-permute-start.5 = (f32[64,1,256]{2,0,1:T(8,128)S(1)}, f32[64,1,256]{2,0,1:T(8,128)S(1)}, u32[]{:S(2)}, u32[]{:S(2)}) collective-permute-start(f32[64,1,256]{2,0,1:T(8,128)S(1)} %bitcast.1049), channel_id=1, source_target_pairs={{1,0},{0,1},{3,2},{2,3},{5,4},{4,5},{7,6},{6,7},{9,8},{8,9},{11,10... | collective-permute-start | bytes 196616 | tf_op jit(solution)/shard_map/ppermute | solution.py:21
  21.3 24.4 %collective-permute-start.4 = (f32[64,1,256]{2,0,1:T(8,128)S(1)}, f32[64,1,256]{2,0,1:T(8,128)S(1)}, u32[]{:S(2)}, u32[]{:S(2)}) collective-permute-start(f32[64,1,256]{2,0,1:T(8,128)S(1)} %bitcast.1050), channel_id=1, source_target_pairs={{0,1},{1,0},{2,3},{3,2},{4,5},{5,4},{6,7},{7,6},{8,9},{9,8},{10,11... | collective-permute-start | bytes 196616 | tf_op jit(solution)/shard_map/ppermute | solution.py:20
  114.9 46.3 %collective-permute-start.7 = (f32[1,1,1024]{2,1,0:T(1,128)S(1)}, f32[1,1,1024]{2,1,0:T(1,128)S(1)}, u32[]{:S(2)}, u32[]{:S(2)}) collective-permute-start(f32[1,1,1024]{2,1,0:T(1,128)S(1)} %get-tuple-element.1124), channel_id=1, source_target_pairs={{0,1},{1,0},{2,3},{3,2},{4,5},{5,4},{6,7},{7,6},{8,9},{9,8},{10,11... | collective-permute-start | bytes 12296 | tf_op jit(solution)/shard_map/ppermute | solution.py:20
  115.0 46.2 %collective-permute-start.6 = (f32[1,1,1024]{2,1,0:T(1,128)S(1)}, f32[1,1,1024]{2,1,0:T(1,128)S(1)}, u32[]{:S(2)}, u32[]{:S(2)}) collective-permute-start(f32[1,1,1024]{2,1,0:T(1,128)S(1)} %get-tuple-element.1125), channel_id=1, source_target_pairs={{1,0},{0,1},{3,2},{2,3},{5,4},{4,5},{7,6},{6,7},{9,8},{8,9},{11,10... | collective-permute-start | bytes 12296 | tf_op jit(solution)/shard_map/ppermute | solution.py:21
  162.1 1.3 collective-permute-start.8
  216.6 1.3 collective-permute-start.15
  216.6 1.3 collective-permute-start.14
  222.3 51.1 %collective-permute-start.21 = (f32[1,1,1024]{2,1,0:T(1,128)S(1)}, f32[1,1,1024]{2,1,0:T(1,128)S(1)}, u32[]{:S(2)}, u32[]{:S(2)}) collective-permute-start(f32[1,1,1024]{2,1,0:T(1,128)S(1)} %get-tuple-element.1079), channel_id=1, source_target_pairs={{0,1},{1,0},{2,3},{3,2},{4,5},{5,4},{6,7},{7,6},{8,9},{9,8},{10,11... | collective-permute-start | bytes 12296 | tf_op jit(solution)/shard_map/ppermute | solution.py:20
  222.6 50.8 %collective-permute-start.20 = (f32[1,1,1024]{2,1,0:T(1,128)S(1)}, f32[1,1,1024]{2,1,0:T(1,128)S(1)}, u32[]{:S(2)}, u32[]{:S(2)}) collective-permute-start(f32[1,1,1024]{2,1,0:T(1,128)S(1)} %get-tuple-element.1080), channel_id=1, source_target_pairs={{1,0},{0,1},{3,2},{2,3},{5,4},{4,5},{7,6},{6,7},{9,8},{8,9},{11,10... | collective-permute-start | bytes 12296 | tf_op jit(solution)/shard_map/ppermute | solution.py:21
  223.4 1.2 collective-permute-start.24
  225.1 1.2 collective-permute-start.26
  273.8 50.9 %collective-permute-start.30 = (f32[2,1,1024]{2,1,0:T(1,128)S(1)}, f32[2,1,1024]{2,1,0:T(1,128)S(1)}, u32[]{:S(2)}, u32[]{:S(2)}) collective-permute-start(f32[2,1,1024]{2,1,0:T(1,128)S(1)} %get-tuple-element.1065), channel_id=1, source_target_pairs={{1,0},{0,1},{3,2},{2,3},{5,4},{4,5},{7,6},{6,7},{9,8},{8,9},{11,10... | collective-permute-start | bytes 24584 | tf_op jit(solution)/shard_map/ppermute | solution.py:21
  273.9 50.8 %collective-permute-start.31 = (f32[2,1,1024]{2,1,0:T(1,128)S(1)}, f32[2,1,1024]{2,1,0:T(1,128)S(1)}, u32[]{:S(2)}, u32[]{:S(2)}) collective-permute-start(f32[2,1,1024]{2,1,0:T(1,128)S(1)} %get-tuple-element.1066), channel_id=1, source_target_pairs={{0,1},{1,0},{2,3},{3,2},{4,5},{5,4},{6,7},{7,6},{8,9},{9,8},{10,11... | collective-permute-start | bytes 24584 | tf_op jit(solution)/shard_map/ppermute | solution.py:20
  325.1 1.2 collective-permute-start.32
  325.1 1.3 collective-permute-start.33
  326.8 1.2 collective-permute-start.34
  375.4 1.9 collective-permute-start.39
  375.4 2.0 collective-permute-start.38
  380.2 3.2 collective-permute-start.41
  380.3 3.1 collective-permute-start.40
  (32 other events, 32.4 us)
Sparse Core Ops, SparseCore 0:
  383.5 89.0 all-reduce.3
where the time goes:
time: 482 us; the launch traced here: 481 us
  blocking collectives  282 us (59%)
  local copies, waits for them, and re-layouts  65.4 us (14%)
  other arithmetic  38.6 us (8%)
  waiting for transfers between devices  35.6 us (7%)
  loops' own time  16.6 us (3%)
  matrix products  15.5 us (3%)
  between operations  15.5 us (3%)
  starting transfers between devices  12 us (2%)
    all_gather x7, blocking collectives, entering(): pieces = jax.tree.map(lambda part: lax.all_gather(part, axis), value)  199 us
    psum x1, blocking collectives, per_device(): lax.psum((grad_first, grad_bias_first, grad_middle, grad_bias_middle, gra...  59.8 us
    select_n x63, other arithmetic, step(): jnp.where(position < mine, new, old)  28.4 us
    dynamic_slice x63, local copies, waits for them, and re-layouts, step(): longer = join(running, jax.tree.map(lambda part: part[position], pieces))  25.1 us
    psum x1, waiting for transfers between devices, per_device(): lax.psum((grad_first, grad_bias_first, grad_middle, grad_bias_middle, gra...  25 us
    unnamed x1, blocking collectives  22.8 us
    broadcast_in_dim x188, local copies, waits for them, and re-layouts, prolong(): return jnp.repeat(jnp.repeat(coarse, 4, axis=-2), 4, axis=-1)  19.9 us
    another operation x6, loops' own time, entering(): return lax.fori_loop(0, count - 1, step, running)  16.6 us
  transfers between devices with their start and end apart: 43, of which 28 were waited for; matrix products, arithmetic and copies ran while one was open for 11% of the time, Pallas kernels for 0%

commit v1 on v0

v1 whole, which is shorter than its diff:
```python
import functools

import jax
import jax.numpy as jnp
from jax import lax
from jax.experimental import pallas as pl
from jax.experimental.pallas import tpu as pltpu
from jax.sharding import PartitionSpec as P

f32, bf16 = jnp.float32, jnp.bfloat16
MESH = pl.DeviceIdType.MESH
CB = 256
CW = 512
OWNERS = 8


def roll(x, shift, axis):
    return pltpu.roll(x, shift % x.shape[axis], axis)


def iota(shape, dim):
    return lax.broadcasted_iota(jnp.int32, shape, dim)


def split(x):
    high = x.astype(bf16)
    return high, (x - high.astype(f32)).astype(bf16)


def dot(a, b, dims):
    return lax.dot_general(a, b, (dims, ((), ())), preferred_element_type=f32)


def dot3(a, b, dims):
    (ah, al), (bh, bl) = a, b
    return dot(ah, bh, dims) + (dot(ah, bl, dims) + dot(al, bh, dims))


NN = ((1,), (0,))
NT = ((1,), (1,))


def east(f):
    return jnp.concatenate([f[..., CB:], roll(f[..., :CB], -1, f.ndim - 1)], axis=-1)


def west(f):
    return jnp.concatenate([roll(f[..., 3 * CB :], 1, f.ndim - 1), f[..., : 3 * CB]], axis=-1)


def step(f, co):
    up, dn, ea, we = co
    ax = f.ndim - 2
    return (0.6 * f + (up * roll(f, -1, ax) + dn * roll(f, 1, ax))) + (ea * east(f) + we * west(f))


def step_t(f, co):
    up, dn, ea, we = co
    ax = f.ndim - 2
    return (0.6 * f + (roll(up * f, 1, ax) + roll(dn * f, -1, ax))) + (west(ea * f) + east(we * f))


def restrict(f):
    z = (f[:, :CB] + f[:, CB : 2 * CB]) + (f[:, 2 * CB : 3 * CB] + f[:, 3 * CB :])
    z = z + roll(z, -1, 0)
    z = (z + roll(z, -2, 0)) * (1.0 / 16.0)
    return jnp.concatenate([z[0:1], z[4:5]], axis=1)


def swap(x):
    return jnp.concatenate([x[:, CB:], x[:, :CB]], axis=1)


def col(x, d):
    if d == 0:
        return x
    return jnp.concatenate([roll(x[:, :CB], -d, 1), roll(x[:, CB:], -d, 1)], axis=1)


def stack(x):
    return jnp.concatenate([col(x, -1), x, col(x, 1)], axis=0)


def apply_k(x, ca, cb):
    reach = len(ca) // 2
    y = swap(x)
    out = None
    for d in range(-reach, reach + 1):
        term = ca[d + reach] * col(x, d) + cb[d + reach] * col(y, d)
        out = term if out is None else out + term
    return out


def apply_kt(x, ca, cb):
    reach = len(ca) // 2
    out = None
    for d in range(-reach, reach + 1):
        term = col(ca[d + reach] * x + swap(cb[d + reach] * x), -d)
        out = term if out is None else out + term
    return out


def probes(co):
    b = iota((8, 4 * CB), 1) % CB
    band = iota((8, 4 * CB), 0) // 4
    lane = iota((1, CW), 1)
    j, first = lane % CB, lane < CB

    def pair(fields):
        r0, r1 = restrict(fields[0]), restrict(fields[1])
        return jnp.where(first, r0, r1), jnp.where(first, r1, r0)

    c4 = [[jnp.zeros((1, CW), f32) for _ in range(3)] for _ in range(2)]
    c8 = [[jnp.zeros((1, CW), f32) for _ in range(5)] for _ in range(2)]

    def put(c, values, color, period):
        reach = len(c[0]) // 2
        for kind in range(2):
            for d in range(-reach, reach + 1):
                here = (j + (d + period)) % period == color
                c[kind][d + reach] = jnp.where(here, values[kind], c[kind][d + reach])

    for p in range(4):
        fields = [jnp.where((b % 4 == p) & (band == i), 1.0, 0.0).astype(f32) for i in range(2)]
        for _ in range(4):
            fields = [step(f, co) for f in fields]
        put(c4, pair(fields), p, 4)
        for p8 in (p, p + 4):
            near = (b + (9 - p8)) % 8 <= 2
            wide = [jnp.where(near, f, 0.0) for f in fields]
            for _ in range(4):
                wide = [step(f, co) for f in wide]
            put(c8, pair(wide), p8, 8)
    return c4, c8


def down(x, first):
    row = iota(x.shape, 0)
    return jnp.where(row == 0, first, roll(x, 1, 0))


def upward(x):
    row = iota(x.shape, 0)
    return jnp.where(row == x.shape[0] - 1, 0.0, roll(x, -1, 0))


def scanner(d, reverse):
    n = d.shape[0]
    row = iota(d.shape, 0)
    levels, k = [], 1
    while k < n:
        shift, ok = (-k, row < n - k) if reverse else (k, row >= k)
        levels.append((k, jnp.where(ok, d, 0.0)))
        d = d * jnp.where(ok, roll(d, shift, 0), 1.0)
        k *= 2

    def run(u):
        for k, factor in levels:
            u = u + factor * roll(u, -k if reverse else k, 0)
        return u

    return run


def sweeps(parts, r_init, a4_init, a8_init, k4, k8):
    d, src, s1, s2, q0, q1, q2 = parts
    row = iota(d.shape, 0)
    forward, backward = scanner(d, False), scanner(d, True)
    c0_next = forward(src + jnp.where(row == 0, d * r_init, 0.0))
    c0 = down(c0_next, r_init)
    rf0 = jnp.where(row == 0, a4_init, apply_k(c0, *k4)) + s1
    e1_next = forward(rf0 - c0_next)
    e1 = down(e1_next, 0.0)
    de1 = d * e1
    w = apply_k(de1, *k4) + jnp.where(row == 0, a8_init, apply_k(c0, *k8)) + s2
    rf1 = down(w, a4_init) + s1
    e2 = down(forward(rf1 - rf0 - de1), 0.0)

    lam = upward(backward(d * q0))
    r2 = q0 + lam
    r1 = upward(backward(q1 + apply_kt(lam, *k4) - d * r2))
    bb = q2 + apply_kt(lam, *k8) + apply_kt(d * (r1 - r2), *k4)
    r0 = upward(backward(upward(bb) - d * r1))
    return c0, e1, e2, r2, r1, r0


def column(row_vector):
    n = row_vector.shape[1]
    eye = iota((n, n), 0) == iota((n, n), 1)
    return jnp.sum(jnp.where(eye, row_vector, 0.0), axis=1, keepdims=True)


def kernel(
    count,
    initial, forcing, vel_x, vel_y, cot,
    w_first, b_first, w_middle, b_middle, w_last, b_last,
    g_first, gb_first, g_middle, gb_middle, g_last, gb_last,
    comb, gat, pack, part, full,
    s0, r0sem, s1sem, r1sem, s2sem, r2sem, s3a, s3b, r3sem,
):
    me, core = lax.axis_index("tm"), lax.axis_index("space")
    other = 1 - core

    def peers(body):
        if count <= 8:
            for d in range(1, count):
                body(lax.rem(me + d, count))
        else:
            lax.fori_loop(1, count, lambda d, c: (body(lax.rem(me + d, count)), c)[1], 0)

    barrier = pltpu.get_barrier_semaphore()

    def greet(t, c):
        pl.semaphore_signal(barrier, inc=1, device_id={"tm": t, "space": c}, device_id_type=MESH)

    greet(me, other)
    peers(lambda t: (greet(t, core), greet(t, other)))

    def remote(src, dst, send, recv, t, c):
        return pltpu.make_async_remote_copy(
            src_ref=src, dst_ref=dst, send_sem=send, recv_sem=recv,
            device_id={"tm": t, "space": c}, device_id_type=MESH,
        )

    def drain(ref, sem):
        pltpu.make_async_copy(ref, ref, sem).wait()

    mine = comb.at[core]
    mine[0] = forcing[0]
    mine[1] = vel_x[...]
    mine[2] = vel_y[...]
    mine[3] = initial[...]
    mine[4] = cot[0]

    mid_a = [w_middle[3 + q] for q in range(3)]
    mid_b = [w_middle[q] + w_middle[6 + q] for q in range(3)]
    mid = split(jnp.concatenate(
        [jnp.concatenate(mid_a, axis=1), jnp.concatenate(mid_b, axis=1)], axis=0))
    mid_t = split(jnp.concatenate(
        [jnp.concatenate([a, b], axis=1) for a, b in zip(mid_a, mid_b)], axis=0).T)
    fst_a = [w_first[3 + q] for q in range(3)]
    fst_b = [w_first[q] + w_first[6 + q] for q in range(3)]
    lst_a = [w_last[3 + q] for q in range(3)]
    lst_b = [w_last[q] + w_last[6 + q] for q in range(3)]
    lst = split(jnp.concatenate(
        [jnp.concatenate(lst_a, axis=1), jnp.concatenate(lst_b, axis=1),
         jnp.zeros((12, 192), f32)], axis=0))
    lst_t = jnp.concatenate(lst_a + lst_b + [jnp.zeros((4, 64), f32)], axis=0).T
    bias1, bias2 = column(b_first[...]), column(b_middle[...])
    src_lane, dst_lane = iota((CW, CW), 0), iota((CW, CW), 1)
    order = jnp.where(src_lane == 4 * (dst_lane % 128) + dst_lane // 128, 1.0, 0.0).astype(bf16)

    pl.semaphore_wait(barrier, 2 * count - 1)
    bands = remote(mine, mine, s0, r0sem, me, other)
    bands.start()
    bands.wait()

    rows = []
    for k in range(5):
        x = jnp.concatenate([comb[0, k], comb[1, k]], axis=0)
        rows += [x[:, :CW], x[:, CW:]]
    x = jnp.concatenate(rows, axis=0)
    high, rest = split(x)
    low = (x - high.astype(f32) - rest.astype(f32)).astype(bf16)
    y = dot(jnp.concatenate([high, rest, low], axis=0), order, NN)
    y = (y[0:80] + y[80:160]) + y[160:240]
    fields = []
    for k in range(5):
        pieces = []
        for s in range(4):
            for h in range(2):
                pieces.append(y[16 * k + 8 * h : 16 * k + 8 * h + 8, 128 * s : 128 * s + 128])
        fields.append(jnp.concatenate(pieces, axis=1))
    force, vx, vy, start, weight = fields

    inputs = [restrict(force), restrict(vx), restrict(vy)]
    pre = jnp.broadcast_to(bias1, (64, CW))
    shifted = [[col(inputs[c], q - 1) for c in range(3)] for q in range(3)]
    for q in range(3):
        for c in range(3):
            v = shifted[q][c]
            pre = pre + (fst_a[q][:, c : c + 1] * v + fst_b[q][:, c : c + 1] * swap(v))
    hidden1 = jnp.tanh(pre)
    stack1 = split(stack(hidden1))
    z = dot3(mid, stack1, NN)
    hidden2 = jnp.tanh(z[:64] + swap(z[64:]) + bias2)
    stack2f = stack(hidden2)
    z = dot3(lst, split(stack2f), NN)
    out = z[0:2] + swap(z[2:4])
    rate = 3.0 / count
    gate = 1.0 / (1.0 + jnp.exp(-(out[0:1] + b_last[0:1, 0:1])))
    decay = jnp.exp(-rate * gate)
    source = (out[1:2] + b_last[0:1, 1:2]) * (1.0 / count)

    co = (0.1 - 0.25 * vy, 0.1 + 0.25 * vy, 0.1 - 0.25 * vx, 0.1 + 0.25 * vx)
    half = 0.5 * force
    sf, av, tv = half, start, weight
    for _ in range(3):
        sf = step(sf, co) + half
    s1 = restrict(sf)
    q0 = restrict(weight)
    for _ in range(4):
        sf, tv = step(sf, co), step_t(tv, co)
    s2, q1 = restrict(sf), restrict(tv)
    for _ in range(4):
        tv = step_t(tv, co)
    q2 = restrict(tv)

    gat[me] = jnp.concatenate(
        [decay, source, s1, s2, q0, q1, q2, jnp.zeros((1, CW), f32)], axis=0)
    peers(lambda t: remote(gat.at[me], gat.at[me], s1sem, r1sem, t, core).start())

    r_init = restrict(start)
    for _ in range(4):
        av = step(av, co)
    a4_init = restrict(av)
    for _ in range(4):
        av = step(av, co)
    a8_init = restrict(av)
    k4, k8 = probes(co)

    drain(gat.at[pl.ds(0, count - 1)], r1sem)
    parts = [gat[:, k, :] for k in range(7)]
    results = sweeps(parts, r_init, a4_init, a8_init, k4, k8)
    here = iota((count, CW), 0) == me
    c0, e1, e2, r2, r1, r0 = [
        jnp.sum(jnp.where(here, v, 0.0), axis=0, keepdims=True) for v in results]
    g_decay = 16.0 * (r2 * e2 + r1 * e1 + r0 * c0)
    go = [g_decay * decay * (-rate) * gate * (1.0 - gate), r0 * (16.0 / count)]

    own = core == 0

    def kind(v):
        return jnp.where(own, v, swap(v))

    grad2 = jnp.zeros((64, CW), f32)
    for q in range(3):
        for o in range(2):
            v = col(go[o], 1 - q)
            at = 2 * q + o
            grad2 = grad2 + (lst_t[:, at : at + 1] * v + lst_t[:, 6 + at : 7 + at] * swap(v))
    grad2 = grad2 * (1.0 - hidden2 * hidden2)
    z = dot3(mid_t, split(jnp.concatenate([col(grad2, 1), grad2, col(grad2, -1)], axis=0)), NN)
    grad1 = (z[:64] + swap(z[64:])) * (1.0 - hidden1 * hidden1)
    gmid = dot3(split(kind(grad2)), stack1, NT)

    def lane_sum(v):
        return jnp.sum(v, axis=1, keepdims=True)

    grad1k = kind(grad1)
    gok = [kind(v) for v in go]
    columns = [lane_sum(grad1k * shifted[q][c]) for q in range(3) for c in range(3)]
    columns += [lane_sum(grad1), lane_sum(grad2)]
    columns += [
        lane_sum(gok[o] * stack2f[64 * q : 64 * q + 64]) for q in range(3) for o in range(2)]
    columns += [jnp.broadcast_to(lane_sum(v), (64, 1)) for v in go]
    lane = iota((64, 64), 1)
    tail = jnp.zeros((64, 64), f32)
    for k, v in enumerate(columns):
        tail = jnp.where(lane == k, v, tail)
    pack[...] = jnp.concatenate([gmid, tail], axis=1)

    def to_owner(t):
        return remote(pack.at[pl.ds(8 * t, 8)], part.at[me], s2sem, r2sem, t, core)

    def spread(body):
        if count == OWNERS:
            body()
        else:
            pl.when(me < OWNERS)(body)

    if count == OWNERS:
        peers(lambda t: to_owner(t).start())
        drain(part.at[pl.ds(0, count - 1)], r2sem)
    else:
        for t in range(OWNERS):
            pl.when(me != t)(lambda t=t: to_owner(t).start())
        spread(lambda: drain(part.at[pl.ds(0, count - 1)], r2sem))

    def publish():
        at = pl.multiple_of(8 * me, 8)
        part[me] = pack[pl.ds(at, 8)]
        total = part[0]
        if count <= 8:
            for t in range(1, count):
                total = total + part[t]
        else:
            total = lax.fori_loop(1, count, lambda t, acc: acc + part[t], total)
        shard = full.at[pl.ds(pl.multiple_of(64 * core + 8 * me, 8), 8)]
        shard[...] = total
        remote(shard, shard, s3b, r3sem, me, other).start()
        peers(lambda t: (remote(shard, shard, s3a, r3sem, t, core).start(),
                         remote(shard, shard, s3b, r3sem, t, other).start()))

    spread(publish)
    if count == OWNERS:
        drain(full.at[pl.ds(0, 120)], r3sem)
    else:
        pl.when(me < OWNERS)(lambda: drain(full.at[pl.ds(0, 120)], r3sem))
        pl.when(me >= OWNERS)(lambda: drain(full, r3sem))

    for k in range(2):
        taps = (1,) if k == 0 else (0, 2)
        grads = full[64 * k : 64 * k + 64, :]
        turned = grads[:, 128:].T
        for q in range(3):
            for p in taps:
                g_middle[3 * p + q] = grads[:, 64 * q : 64 * q + 64]
                g_first[3 * p + q] = grads[:, 192 + 3 * q : 195 + 3 * q]
                g_last[3 * p + q] = turned[75 + 2 * q : 77 + 2 * q, :]
        if k == 0:
            gb_first[...] = turned[73:74, :]
            gb_middle[...] = turned[74:75, :]
            gb_last[...] = grads[0:1, 209:211]

    drain(gat.at[pl.ds(0, count - 1)], s1sem)
    if count == OWNERS:
        drain(part.at[pl.ds(0, count - 1)], s2sem)
    else:
        pl.when(me < OWNERS)(lambda: drain(pack.at[pl.ds(0, 56)], s2sem))
        pl.when(me >= OWNERS)(lambda: drain(pack, s2sem))

    def sent():
        drain(part.at[pl.ds(0, count - 1)], s3a)
        drain(part, s3b)

    spread(sent)


def per_device(count, *args):
    initial, forcing, vx, vy, cot, w1, b1, w2, b2, w3, b3 = args
    vmem = pl.BlockSpec(memory_space=pltpu.VMEM)
    dma = pltpu.SemaphoreType.DMA
    outs = pl.pallas_call(
        functools.partial(kernel, count),
        out_shape=[
            jax.ShapeDtypeStruct(s, f32)
            for s in ((9, 64, 3), (1, 64), (9, 64, 64), (1, 64), (9, 2, 64), (1, 2))],
        in_specs=[vmem] * 11,
        out_specs=[vmem] * 6,
        scratch_shapes=[
            pltpu.VMEM((2, 5, 4, 1024), f32),
            pltpu.VMEM((count, 8, CW), f32),
            pltpu.VMEM((64, 256), f32),
            pltpu.VMEM((count, 8, 256), f32),
            pltpu.VMEM((128, 256), f32),
        ] + [dma] * 9,
        compiler_params=pltpu.CompilerParams(
            collective_id=0, has_side_effects=True, vmem_limit_bytes=40 * 1024 * 1024),
    )(initial, forcing, vx, vy, cot, w1, b1.reshape(1, 64), w2, b2.reshape(1, 64), w3,
      b3.reshape(1, 2))
    return (outs[0], outs[1].reshape(64), outs[2], outs[3].reshape(64), outs[4],
            outs[5].reshape(2))


def solution(mesh):
    band, piece = P(("groups", "space"), None), P(("groups", "tm"), "space", None)
    return jax.shard_map(
        functools.partial(per_device, mesh.shape["tm"]),
        mesh=mesh,
        in_specs=(band, piece, band, band, piece) + (P(),) * 6,
        out_specs=(
            P("groups", None, None), P("groups"), P("groups", None, None), P("groups"),
            P("groups", None, None), P("groups"),
        ),
        check_vma=False,
    )
```

time: 482 us -> 33.1 us (0.07)
  blocking collectives: 282 us -> 0 us
  local copies, waits for them, and re-layouts: 65.4 us -> 8.1 us
  other arithmetic: 38.6 us -> 0 us
  waiting for transfers between devices: 35.6 us -> 0 us
  Pallas kernels: 0 us -> 23.7 us
  loops' own time: 16.6 us -> 0 us
  matrix products: 15.5 us -> 0 us
  between operations: 15.5 us -> 0.74 us
  starting transfers between devices: 12 us -> 0 us
    all_gather x7 -> x0, blocking collectives: 199 us -> none  [entering(): pieces = jax.tree.map(lambda part: lax.all_gather(part, axis), value)]
    psum x1 -> x0, blocking collectives: 59.8 us -> none  [per_device(): lax.psum((grad_first, grad_bias_first, grad_middle, grad_bias_middle, gra...]
    select_n x63 -> x0, other arithmetic: 28.4 us -> none  [step(): jnp.where(position < mine, new, old)]
    dynamic_slice x63 -> x0, local copies, waits for them, and re-layouts: 25.1 us -> none  [step(): longer = join(running, jax.tree.map(lambda part: part[position], pieces))]
    psum x1 -> x0, waiting for transfers between devices: 25 us -> none  [per_device(): lax.psum((grad_first, grad_bias_first, grad_middle, grad_bias_middle, gra...]
    pallas_call x0 -> x1, Pallas kernels: none -> 23.7 us  [per_device(): pl.pallas_call(functools.partial(kernel, count), out_shape=[jax.ShapeDtyp...]
    unnamed x1 -> x0, blocking collectives: 22.8 us -> none
    broadcast_in_dim x188 -> x0, local copies, waits for them, and re-layouts: 19.9 us -> none  [prolong(): return jnp.repeat(jnp.repeat(coarse, 4, axis=-2), 4, axis=-1)]
  transfers between devices with their start and end apart: 43 -> 0, of which waited for: 28 -> 0; matrix products, arithmetic and copies ran while one was open for 11% -> 0% of each run, Pallas kernels for 0% -> 0%
where the time goes in v1:
time: 33.1 us; the launch traced here: 32.5 us
  Pallas kernels  23.7 us (72%)
  local copies, waits for them, and re-layouts  8.1 us (24%)
  between operations  0.74 us (2%)
    pallas_call x1, Pallas kernels, per_device(): pl.pallas_call(functools.partial(kernel, count), out_shape=[jax.ShapeDtyp...  23.7 us
    unnamed x27, local copies, waits for them, and re-layouts  8.1 us

profile of v1, /device:TPU:0, one launch (start us, length us, event | category | flops | bytes accessed | tf_op | source)
XLA Modules:
  0.0 32.5 jit_solution(3979629669521313311)
XLA Ops:
  0.6 0.0 copy-start
  0.6 0.0 copy-start.1
  0.7 0.0 copy-start.7
  0.7 0.0 copy-start.8
  0.7 0.0 copy-start.9
  0.7 0.9 %copy.17.w_first = f32[9,64,3]{2,1,0:T(8,128)S(1)} copy(f32[9,64,3]{1,2,0:T(4,128)} %param.16) | data formatting | bytes 13824 | tf_op args[5]
  1.6 0.0 copy-done
  1.6 0.0 copy-done.1
  1.6 0.0 copy-done.7
  1.6 0.0 copy-done.8
  1.6 0.0 copy-done.9
  1.7 0.0 copy-start.2
  1.7 0.7 %copy-done.2 = f32[1,4,1024]{2,1,0:T(4,128)S(1)} copy-done((f32[1,4,1024]{2,1,0:T(4,128)S(1)}, f32[1,4,1024]{2,1,0:T(4,128)}, u32[]{:S(2)}) %copy-start.2) | copy-done | bytes 16408
  2.4 0.7 %copy-done.3 = f32[4,1024]{1,0:T(4,128)S(1)} copy-done((f32[4,1024]{1,0:T(4,128)S(1)}, f32[4,1024]{1,0:T(4,128)}, u32[]{:S(2)}) %copy-start.3) | copy-done | bytes 16408
  3.1 0.7 %copy-done.4 = f32[4,1024]{1,0:T(4,128)S(1)} copy-done((f32[4,1024]{1,0:T(4,128)S(1)}, f32[4,1024]{1,0:T(4,128)}, u32[]{:S(2)}) %copy-start.4) | copy-done | bytes 16408
  3.8 0.7 %copy-done.5 = f32[1,4,1024]{2,1,0:T(4,128)S(1)} copy-done((f32[1,4,1024]{2,1,0:T(4,128)S(1)}, f32[1,4,1024]{2,1,0:T(4,128)}, u32[]{:S(2)}) %copy-start.5) | copy-done | bytes 16408
  4.5 0.7 %copy-done.6 = f32[9,2,64]{2,1,0:T(2,128)S(1)} copy-done((f32[9,2,64]{2,1,0:T(2,128)S(1)}, f32[9,2,64]{2,1,0:T(2,128)}, u32[]{:S(2)}) %copy-start.6) | copy-done | bytes 4632
  5.2 23.7 %shard_map.154 = (f32[9,64,3]{2,1,0:T(8,128)S(1)}, f32[1,64]{1,0:T(1,128)S(1)}, f32[9,64,64]{2,1,0:T(8,128)S(1)}, f32[1,64]{1,0:T(1,128)S(1)}, f32[9,2,64]{2,1,0:T(2,128)S(1)}, /*index=5*/f32[1,2]{1,0:T(1,128)S(1)}) custom-call(f32[4,1024]{1,0:T(4,128)S(1)} %copy-done.1, f32[1,4,1024]{2,1,0:T(4,128)S(1)} %copy-done.2, f32[4,1024]{1,0:T(4,128)S(1)} %copy-done.3, ...), custom_call_target="tpu_custom_call" | custom-call | tf_op jit(solution)/shard_map/pallas_call | solution.py:434
  29.0 0.8 %copy.18 = f32[9,64,3]{1,2,0:T(4,128)} copy(f32[9,64,3]{2,1,0:T(8,128)S(1)} %get-tuple-element.18) | data formatting | bytes 13824
  29.7 0.5 %copy.24 = f32[64]{0:T(128)} copy(f32[64]{0:T(128)S(1)} %bitcast.11) | data formatting | bytes 512
  30.2 0.7 %copy.25 = f32[9,64,64]{2,1,0:T(8,128)} copy(f32[9,64,64]{2,1,0:T(8,128)S(1)} %get-tuple-element.32) | data formatting | bytes 294912
  30.9 0.5 %copy.26 = f32[64]{0:T(128)} copy(f32[64]{0:T(128)S(1)} %bitcast.10) | data formatting | bytes 512
  31.4 0.6 %copy.27 = f32[9,2,64]{2,1,0:T(2,128)} copy(f32[9,2,64]{2,1,0:T(2,128)S(1)} %get-tuple-element.34) | data formatting | bytes 9216
  32.0 0.5 %copy.28 = f32[2]{0:T(128)} copy(f32[2]{0:T(128)S(1)} %bitcast.9) | data formatting | bytes 16
  (4 shorter events, 0.0 us)
Async XLA Ops:
  0.6 1.0 %copy-start = (f32[9,64,64]{2,1,0:T(8,128)S(1)}, f32[9,64,64]{2,1,0:T(8,128)}, u32[]{:S(2)}) copy-start(f32[9,64,64]{2,1,0:T(8,128)} %w_middle.1) | copy-start | bytes 442372
  0.6 1.0 %copy-start.1 = (f32[4,1024]{1,0:T(4,128)S(1)}, f32[4,1024]{1,0:T(4,128)}, u32[]{:S(2)}) copy-start(f32[4,1024]{1,0:T(4,128)} %initial.1) | copy-start | bytes 49156
  0.7 1.0 %copy-start.7 = (f32[64]{0:T(128)S(1)}, f32[64]{0:T(128)}, u32[]{:S(2)}) copy-start(f32[64]{0:T(128)} %param.17) | copy-start | bytes 772
  0.7 1.0 %copy-start.8 = (f32[64]{0:T(128)S(1)}, f32[64]{0:T(128)}, u32[]{:S(2)}) copy-start(f32[64]{0:T(128)} %param.19) | copy-start | bytes 772
  0.7 1.0 %copy-start.9 = (f32[2]{0:T(128)S(1)}, f32[2]{0:T(128)}, u32[]{:S(2)}) copy-start(f32[2]{0:T(128)} %param.21) | copy-start | bytes 28
  1.7 0.7 %copy-start.2 = (f32[1,4,1024]{2,1,0:T(4,128)S(1)}, f32[1,4,1024]{2,1,0:T(4,128)}, u32[]{:S(2)}) copy-start(f32[1,4,1024]{2,1,0:T(4,128)} %forcing.1) | copy-start | bytes 49156
  2.4 0.7 %copy-start.3 = (f32[4,1024]{1,0:T(4,128)S(1)}, f32[4,1024]{1,0:T(4,128)}, u32[]{:S(2)}) copy-start(f32[4,1024]{1,0:T(4,128)} %vel_x.1) | copy-start | bytes 49156
  3.1 0.7 %copy-start.4 = (f32[4,1024]{1,0:T(4,128)S(1)}, f32[4,1024]{1,0:T(4,128)}, u32[]{:S(2)}) copy-start(f32[4,1024]{1,0:T(4,128)} %vel_y.1) | copy-start | bytes 49156
  3.8 0.7 %copy-start.5 = (f32[1,4,1024]{2,1,0:T(4,128)S(1)}, f32[1,4,1024]{2,1,0:T(4,128)}, u32[]{:S(2)}) copy-start(f32[1,4,1024]{2,1,0:T(4,128)} %cot.1) | copy-start | bytes 49156
  4.5 0.7 %copy-start.6 = (f32[9,2,64]{2,1,0:T(2,128)S(1)}, f32[9,2,64]{2,1,0:T(2,128)}, u32[]{:S(2)}) copy-start(f32[9,2,64]{2,1,0:T(2,128)} %w_last.1) | copy-start | bytes 13828

commit v2 on v1

--- a/solution.py
+++ b/solution.py
@@ -184,19 +184,14 @@
     return c0, e1, e2, r2, r1, r0
 
 
-def column(row_vector):
-    n = row_vector.shape[1]
-    eye = iota((n, n), 0) == iota((n, n), 1)
-    return jnp.sum(jnp.where(eye, row_vector, 0.0), axis=1, keepdims=True)
-
-
 def kernel(
     count,
     initial, forcing, vel_x, vel_y, cot,
-    w_first, b_first, w_middle, b_middle, w_last, b_last,
-    g_first, gb_first, g_middle, gb_middle, g_last, gb_last,
+    first_hbm, bias1_hbm, middle_hbm, bias2_hbm, last_hbm, bias3_hbm,
+    result,
+    w1, b1, w_middle, b2, w3, b3,
     comb, gat, pack, part, full,
-    s0, r0sem, s1sem, r1sem, s2sem, r2sem, s3a, s3b, r3sem,
+    s0, r0sem, s1sem, r1sem, s2sem, r2sem, s3a, s3b, r3sem, band_sem, weight_sem,
 ):
     me, core = lax.axis_index("tm"), lax.axis_index("space")
     other = 1 - core
@@ -208,6 +203,17 @@
         else:
             lax.fori_loop(1, count, lambda d, c: (body(lax.rem(me + d, count)), c)[1], 0)
 
+    mine = comb.at[core]
+    for k, ref in enumerate((forcing.at[0], vel_x, vel_y, initial, cot.at[0])):
+        pltpu.make_async_copy(ref, mine.at[k], band_sem).start()
+    loads = [
+        pltpu.make_async_copy(src, dst, weight_sem.at[k])
+        for k, (src, dst) in enumerate((
+            (first_hbm, w1), (bias1_hbm, b1), (middle_hbm, w_middle), (bias2_hbm, b2),
+            (last_hbm, w3), (bias3_hbm, b3)))]
+    for load in loads:
+        load.start()
+
     barrier = pltpu.get_barrier_semaphore()
 
     def greet(t, c):
@@ -225,12 +231,8 @@
     def drain(ref, sem):
         pltpu.make_async_copy(ref, ref, sem).wait()
 
-    mine = comb.at[core]
-    mine[0] = forcing[0]
-    mine[1] = vel_x[...]
-    mine[2] = vel_y[...]
-    mine[3] = initial[...]
-    mine[4] = cot[0]
+    for load in loads:
+        load.wait()
 
     mid_a = [w_middle[3 + q] for q in range(3)]
     mid_b = [w_middle[q] + w_middle[6 + q] for q in range(3)]
@@ -238,19 +240,21 @@
         [jnp.concatenate(mid_a, axis=1), jnp.concatenate(mid_b, axis=1)], axis=0))
     mid_t = split(jnp.concatenate(
         [jnp.concatenate([a, b], axis=1) for a, b in zip(mid_a, mid_b)], axis=0).T)
-    fst_a = [w_first[3 + q] for q in range(3)]
-    fst_b = [w_first[q] + w_first[6 + q] for q in range(3)]
-    lst_a = [w_last[3 + q] for q in range(3)]
-    lst_b = [w_last[q] + w_last[6 + q] for q in range(3)]
+    fst_a = [w1[3 + q] for q in range(3)]
+    fst_b = [w1[q] + w1[6 + q] for q in range(3)]
+    lst_a = [w3[3 + q] for q in range(3)]
+    lst_b = [w3[q] + w3[6 + q] for q in range(3)]
     lst = split(jnp.concatenate(
         [jnp.concatenate(lst_a, axis=1), jnp.concatenate(lst_b, axis=1),
          jnp.zeros((12, 192), f32)], axis=0))
-    lst_t = jnp.concatenate(lst_a + lst_b + [jnp.zeros((4, 64), f32)], axis=0).T
-    bias1, bias2 = column(b_first[...]), column(b_middle[...])
+    upright = jnp.concatenate(fst_a + fst_b + lst_a + lst_b + [b1[...], b2[...]], axis=0).T
+    bias1, bias2 = upright[:, 30:31], upright[:, 31:32]
+    b_last = b3[...]
     src_lane, dst_lane = iota((CW, CW), 0), iota((CW, CW), 1)
     order = jnp.where(src_lane == 4 * (dst_lane % 128) + dst_lane // 128, 1.0, 0.0).astype(bf16)
 
     pl.semaphore_wait(barrier, 2 * count - 1)
+    drain(mine, band_sem)
     bands = remote(mine, mine, s0, r0sem, me, other)
     bands.start()
     bands.wait()
@@ -279,7 +283,8 @@
     for q in range(3):
         for c in range(3):
             v = shifted[q][c]
-            pre = pre + (fst_a[q][:, c : c + 1] * v + fst_b[q][:, c : c + 1] * swap(v))
+            pre = pre + (upright[:, 3 * q + c : 3 * q + c + 1] * v
+                         + upright[:, 9 + 3 * q + c : 10 + 3 * q + c] * swap(v))
     hidden1 = jnp.tanh(pre)
     stack1 = split(stack(hidden1))
     z = dot3(mid, stack1, NN)
@@ -337,8 +342,9 @@
     for q in range(3):
         for o in range(2):
             v = col(go[o], 1 - q)
-            at = 2 * q + o
-            grad2 = grad2 + (lst_t[:, at : at + 1] * v + lst_t[:, 6 + at : 7 + at] * swap(v))
+            at = 18 + 2 * q + o
+            grad2 = grad2 + (
+                upright[:, at : at + 1] * v + upright[:, 6 + at : 7 + at] * swap(v))
     grad2 = grad2 * (1.0 - hidden2 * hidden2)
     z = dot3(mid_t, split(jnp.concatenate([col(grad2, 1), grad2, col(grad2, -1)], axis=0)), NN)
     grad1 = (z[:64] + swap(z[64:])) * (1.0 - hidden1 * hidden1)
@@ -399,19 +405,7 @@
         pl.when(me < OWNERS)(lambda: drain(full.at[pl.ds(0, 120)], r3sem))
         pl.when(me >= OWNERS)(lambda: drain(full, r3sem))
 
-    for k in range(2):
-        taps = (1,) if k == 0 else (0, 2)
-        grads = full[64 * k : 64 * k + 64, :]
-        turned = grads[:, 128:].T
-        for q in range(3):
-            for p in taps:
-                g_middle[3 * p + q] = grads[:, 64 * q : 64 * q + 64]
-                g_first[3 * p + q] = grads[:, 192 + 3 * q : 195 + 3 * q]
-                g_last[3 * p + q] = turned[75 + 2 * q : 77 + 2 * q, :]
-        if k == 0:
-            gb_first[...] = turned[73:74, :]
-            gb_middle[...] = turned[74:75, :]
-            gb_last[...] = grads[0:1, 209:211]
+    result[...] = full[...]
 
     drain(gat.at[pl.ds(0, count - 1)], s1sem)
     if count == OWNERS:
@@ -427,30 +421,65 @@
     spread(sent)
 
 
+GRADS = ((9, 3, 64), (1, 64), (9, 64, 64), (1, 64), (9, 2, 64), (1, 2))
+
+
+def unpack(full, *refs):
+    outs, (g_first, gb_first, g_middle, gb_middle, g_last, gb_last), sem = (
+        refs[:6], refs[6:12], refs[12])
+    copies = [pltpu.make_async_copy(refs[6 + k], outs[k], sem.at[k]) for k in range(6)]
+    halves = [full[0:64, :], full[64:128, :]]
+    for k in range(2):
+        for q in range(3):
+            for p in ((1,), (0, 2))[k]:
+                g_middle[3 * p + q] = halves[k][:, 64 * q : 64 * q + 64]
+    copies[2].start()
+    for k in range(2):
+        turned = halves[k][:, 128:].T
+        for q in range(3):
+            for p in ((1,), (0, 2))[k]:
+                g_first[3 * p + q] = turned[64 + 3 * q : 67 + 3 * q, :]
+                g_last[3 * p + q] = turned[75 + 2 * q : 77 + 2 * q, :]
+        if k == 0:
+            gb_first[...] = turned[73:74, :]
+            gb_middle[...] = turned[74:75, :]
+            gb_last[...] = halves[0][0:1, 209:211]
+    for k in (0, 1, 3, 4, 5):
+        copies[k].start()
+    for copy in copies:
+        copy.wait()
+
+
 def per_device(count, *args):
     initial, forcing, vx, vy, cot, w1, b1, w2, b2, w3, b3 = args
-    vmem = pl.BlockSpec(memory_space=pltpu.VMEM)
+    vmem, hbm = pl.BlockSpec(memory_space=pltpu.VMEM), pl.BlockSpec(memory_space=pltpu.HBM)
     dma = pltpu.SemaphoreType.DMA
-    outs = pl.pallas_call(
+    grads = [pltpu.VMEM(s, f32) for s in GRADS]
+    full = pl.pallas_call(
         functools.partial(kernel, count),
-        out_shape=[
-            jax.ShapeDtypeStruct(s, f32)
-            for s in ((9, 64, 3), (1, 64), (9, 64, 64), (1, 64), (9, 2, 64), (1, 2))],
-        in_specs=[vmem] * 11,
-        out_specs=[vmem] * 6,
-        scratch_shapes=[
+        out_shape=jax.ShapeDtypeStruct((128, 256), f32),
+        in_specs=[hbm] * 11,
+        out_specs=vmem,
+        scratch_shapes=grads + [
             pltpu.VMEM((2, 5, 4, 1024), f32),
             pltpu.VMEM((count, 8, CW), f32),
             pltpu.VMEM((64, 256), f32),
             pltpu.VMEM((count, 8, 256), f32),
             pltpu.VMEM((128, 256), f32),
-        ] + [dma] * 9,
+        ] + [dma] * 10 + [dma((6,))],
         compiler_params=pltpu.CompilerParams(
-            collective_id=0, has_side_effects=True, vmem_limit_bytes=40 * 1024 * 1024),
-    )(initial, forcing, vx, vy, cot, w1, b1.reshape(1, 64), w2, b2.reshape(1, 64), w3,
-      b3.reshape(1, 2))
-    return (outs[0], outs[1].reshape(64), outs[2], outs[3].reshape(64), outs[4],
-            outs[5].reshape(2))
+            collective_id=0, has_side_effects=True, vmem_limit_bytes=62 * 1024 * 1024),
+    )(initial, forcing, vx, vy, cot, w1.transpose(0, 2, 1), b1.reshape(1, 64), w2,
+      b2.reshape(1, 64), w3, b3.reshape(1, 2))
+    outs = pl.pallas_call(
+        unpack,
+        out_shape=[jax.ShapeDtypeStruct(s, f32) for s in GRADS],
+        in_specs=[vmem],
+        out_specs=[hbm] * 6,
+        scratch_shapes=grads + [dma((6,))],
+    )(full)
+    return (outs[0].transpose(0, 2, 1), outs[1].reshape(64), outs[2], outs[3].reshape(64),
+            outs[4], outs[5].reshape(2))
 
 
 def solution(mesh):

time: 33.1 us -> 27 us (0.82); the launches traced: 32.5 us -> 26.8 us
  local copies, waits for them, and re-layouts: 8.1 us -> 0 us
  Pallas kernels: 23.7 us -> 26.2 us
    unnamed x27 -> x0, local copies, waits for them, and re-layouts: 8.1 us -> none
    pallas_call x1 -> x2, Pallas kernels: 23.7 us -> 26.2 us  [the longest x1 24.4 us: per_device(): pl.pallas_call(functools.partial(kernel, count), out_shape=jax.ShapeDtype...]
where the time goes in v2:
time: 27 us; the launch traced here: 26.8 us
  Pallas kernels  26.2 us (97%)
  between operations  0.64 us (2%)
    pallas_call x1, Pallas kernels, per_device(): pl.pallas_call(functools.partial(kernel, count), out_shape=jax.ShapeDtype...  24.4 us
    pallas_call x1, Pallas kernels, per_device(): pl.pallas_call(unpack, out_shape=[jax.ShapeDtypeStruct(s, f32) for s in G...  1.76 us

profile of v2, /device:TPU:0, one launch (start us, length us, event | category | flops | bytes accessed | tf_op | source)
XLA Modules:
  0.0 26.8 jit_solution(12189996658935899103)
XLA Ops:
  0.6 24.4 %shard_map.154.full = f32[128,256]{1,0:T(8,128)} custom-call(f32[4,1024]{1,0:T(4,128)} %initial.1, f32[1,4,1024]{2,1,0:T(4,128)} %forcing.1, f32[4,1024]{1,0:T(4,128)} %vel_x.1, f32[4,1024]{1,0:T(4,128)} %vel_y.1, f32[1,4,1024]{2,1,0:T(4,128)} %cot.1, f32[9,3,64]{2,1,0:T(4,128)} %bitcast.8, f32[1,64]{1,0:T(1,128)} %bitcast.9, f32[9,64,64]{2,1,0:T(8,128)} %middle_hbm.1, ...), custom_call_target="tpu_custom_call" | custom-call | tf_op jit(solution)/shard_map/pallas_call | solution.py:458
  25.0 1.8 %shard_map.155 = (f32[9,3,64]{2,1,0:T(4,128)}, f32[1,64]{1,0:T(1,128)}, f32[9,64,64]{2,1,0:T(8,128)}, f32[1,64]{1,0:T(1,128)}, f32[9,2,64]{2,1,0:T(2,128)}, /*index=5*/f32[1,2]{1,0:T(1,128)}) custom-call(f32[128,256]{1,0:T(8,128)} %shard_map.154.full), custom_call_target="tpu_custom_call" | custom-call | tf_op jit(solution)/shard_map/pallas_call | solution.py:474

commit v3 on v2

--- a/solution.py
+++ b/solution.py
@@ -190,7 +190,7 @@
     first_hbm, bias1_hbm, middle_hbm, bias2_hbm, last_hbm, bias3_hbm,
     result,
     w1, b1, w_middle, b2, w3, b3,
-    comb, gat, pack, part, full,
+    raw, comb, gat, pack, part, full,
     s0, r0sem, s1sem, r1sem, s2sem, r2sem, s3a, s3b, r3sem, band_sem, weight_sem,
 ):
     me, core = lax.axis_index("tm"), lax.axis_index("space")
@@ -205,7 +205,7 @@
 
     mine = comb.at[core]
     for k, ref in enumerate((forcing.at[0], vel_x, vel_y, initial, cot.at[0])):
-        pltpu.make_async_copy(ref, mine.at[k], band_sem).start()
+        pltpu.make_async_copy(ref, raw.at[k], band_sem).start()
     loads = [
         pltpu.make_async_copy(src, dst, weight_sem.at[k])
         for k, (src, dst) in enumerate((
@@ -230,6 +230,26 @@
 
     def drain(ref, sem):
         pltpu.make_async_copy(ref, ref, sem).wait()
+
+    src_lane, dst_lane = iota((CW, CW), 0), iota((CW, CW), 1)
+    order = jnp.where(src_lane == 4 * (dst_lane % 128) + dst_lane // 128, 1.0, 0.0).astype(bf16)
+    drain(raw, band_sem)
+    x = jnp.concatenate([raw[k] for k in range(5)] + [jnp.zeros((4, 1024), f32)], axis=0)
+    x = jnp.concatenate([x[:, :CW], x[:, CW:]], axis=0)
+    high, rest = split(x)
+    low = (x - high.astype(f32) - rest.astype(f32)).astype(bf16)
+    y = dot(jnp.concatenate([high, rest, low], axis=0), order, NN)
+    y = (y[0:48] + y[48:96]) + y[96:144]
+    for k in range(5):
+        for s in range(4):
+            for h in range(2):
+                at = CB * s + 128 * h
+                mine[k, :, at : at + 128] = y[
+                    24 * h + 4 * k : 24 * h + 4 * k + 4, 128 * s : 128 * s + 128]
+
+    pl.semaphore_wait(barrier, 2 * count - 1)
+    bands = remote(mine, mine, s0, r0sem, me, other)
+    bands.start()
 
     for load in loads:
         load.wait()
@@ -250,32 +270,10 @@
     upright = jnp.concatenate(fst_a + fst_b + lst_a + lst_b + [b1[...], b2[...]], axis=0).T
     bias1, bias2 = upright[:, 30:31], upright[:, 31:32]
     b_last = b3[...]
-    src_lane, dst_lane = iota((CW, CW), 0), iota((CW, CW), 1)
-    order = jnp.where(src_lane == 4 * (dst_lane % 128) + dst_lane // 128, 1.0, 0.0).astype(bf16)
-
-    pl.semaphore_wait(barrier, 2 * count - 1)
-    drain(mine, band_sem)
-    bands = remote(mine, mine, s0, r0sem, me, other)
-    bands.start()
+
     bands.wait()
-
-    rows = []
-    for k in range(5):
-        x = jnp.concatenate([comb[0, k], comb[1, k]], axis=0)
-        rows += [x[:, :CW], x[:, CW:]]
-    x = jnp.concatenate(rows, axis=0)
-    high, rest = split(x)
-    low = (x - high.astype(f32) - rest.astype(f32)).astype(bf16)
-    y = dot(jnp.concatenate([high, rest, low], axis=0), order, NN)
-    y = (y[0:80] + y[80:160]) + y[160:240]
-    fields = []
-    for k in range(5):
-        pieces = []
-        for s in range(4):
-            for h in range(2):
-                pieces.append(y[16 * k + 8 * h : 16 * k + 8 * h + 8, 128 * s : 128 * s + 128])
-        fields.append(jnp.concatenate(pieces, axis=1))
-    force, vx, vy, start, weight = fields
+    force, vx, vy, start, weight = [
+        jnp.concatenate([comb[0, k], comb[1, k]], axis=0) for k in range(5)]
 
     inputs = [restrict(force), restrict(vx), restrict(vy)]
     pre = jnp.broadcast_to(bias1, (64, CW))
@@ -461,6 +459,7 @@
         in_specs=[hbm] * 11,
         out_specs=vmem,
         scratch_shapes=grads + [
+            pltpu.VMEM((5, 4, 1024), f32),
             pltpu.VMEM((2, 5, 4, 1024), f32),
             pltpu.VMEM((count, 8, CW), f32),
             pltpu.VMEM((64, 256), f32),

time: 27 us -> 27.2 us (level)
  no operation moved by 1% of the time
where the time goes in v3:
time: 27.2 us; the launch traced here: 27 us
  Pallas kernels  26.4 us (97%)
  between operations  0.64 us (2%)
    pallas_call x1, Pallas kernels, per_device(): pl.pallas_call(functools.partial(kernel, count), out_shape=jax.ShapeDtype...  24.6 us
    pallas_call x1, Pallas kernels, per_device(): pl.pallas_call(unpack, out_shape=[jax.ShapeDtypeStruct(s, f32) for s in G...  1.76 us

profile of v3, /device:TPU:0, one launch (start us, length us, event | category | flops | bytes accessed | tf_op | source)
XLA Modules:
  0.0 27.0 jit_solution(664495636522447408)
XLA Ops:
  0.6 24.6 %shard_map.154.full = f32[128,256]{1,0:T(8,128)} custom-call(f32[4,1024]{1,0:T(4,128)} %initial.1, f32[1,4,1024]{2,1,0:T(4,128)} %forcing.1, f32[4,1024]{1,0:T(4,128)} %vel_x.1, f32[4,1024]{1,0:T(4,128)} %vel_y.1, f32[1,4,1024]{2,1,0:T(4,128)} %cot.1, f32[9,3,64]{2,1,0:T(4,128)} %bitcast.8, f32[1,64]{1,0:T(1,128)} %bitcast.9, f32[9,64,64]{2,1,0:T(8,128)} %middle_hbm.1, ...), custom_call_target="tpu_custom_call" | custom-call | tf_op jit(solution)/shard_map/pallas_call | solution.py:456
  25.3 1.8 %shard_map.155 = (f32[9,3,64]{2,1,0:T(4,128)}, f32[1,64]{1,0:T(1,128)}, f32[9,64,64]{2,1,0:T(8,128)}, f32[1,64]{1,0:T(1,128)}, f32[9,2,64]{2,1,0:T(2,128)}, /*index=5*/f32[1,2]{1,0:T(1,128)}) custom-call(f32[128,256]{1,0:T(8,128)} %shard_map.154.full), custom_call_target="tpu_custom_call" | custom-call | tf_op jit(solution)/shard_map/pallas_call | solution.py:473

commit v4 on v3

--- a/solution.py
+++ b/solution.py
@@ -344,9 +344,44 @@
             grad2 = grad2 + (
                 upright[:, at : at + 1] * v + upright[:, 6 + at : 7 + at] * swap(v))
     grad2 = grad2 * (1.0 - hidden2 * hidden2)
+    def to_owner(t, h):
+        return remote(
+            pack.at[h, pl.ds(8 * t, 8)], part.at[h, me], s2sem.at[h], r2sem.at[h], t, core)
+
+    def contribute(h):
+        if count == OWNERS:
+            peers(lambda t: to_owner(t, h).start())
+        else:
+            for t in range(OWNERS):
+                pl.when(me != t)(lambda t=t: to_owner(t, h).start())
+
+    def spread(body):
+        if count == OWNERS:
+            body()
+        else:
+            pl.when(me < OWNERS)(body)
+
+    def publish(h):
+        drain(part.at[h, pl.ds(0, count - 1)], r2sem.at[h])
+        part[h, me] = pack[h, pl.ds(pl.multiple_of(8 * me, 8), 8)]
+        total = part[h, 0]
+        if count <= 8:
+            for t in range(1, count):
+                total = total + part[h, t]
+        else:
+            total = lax.fori_loop(1, count, lambda t, acc: acc + part[h, t], total)
+        shard = full.at[h, pl.ds(pl.multiple_of(64 * core + 8 * me, 8), 8)]
+        shard[...] = total
+        peers(lambda t: (remote(shard, shard, s3a.at[h], r3sem.at[h], t, core).start(),
+                         remote(shard, shard, s3b.at[h], r3sem.at[h], t, other).start()))
+        remote(shard, shard, s3b.at[h], r3sem.at[h], me, other).start()
+
+    gmid = dot3(split(kind(grad2)), stack1, NT)
+    pack[0] = gmid[:, :128]
+    contribute(0)
+
     z = dot3(mid_t, split(jnp.concatenate([col(grad2, 1), grad2, col(grad2, -1)], axis=0)), NN)
     grad1 = (z[:64] + swap(z[64:])) * (1.0 - hidden1 * hidden1)
-    gmid = dot3(split(kind(grad2)), stack1, NT)
 
     def lane_sum(v):
         return jnp.sum(v, axis=1, keepdims=True)
@@ -362,61 +397,33 @@
     tail = jnp.zeros((64, 64), f32)
     for k, v in enumerate(columns):
         tail = jnp.where(lane == k, v, tail)
-    pack[...] = jnp.concatenate([gmid, tail], axis=1)
-
-    def to_owner(t):
-        return remote(pack.at[pl.ds(8 * t, 8)], part.at[me], s2sem, r2sem, t, core)
-
-    def spread(body):
+    pack[1] = jnp.concatenate([gmid[:, 128:], tail], axis=1)
+    contribute(1)
+    for h in range(2):
+        spread(lambda: publish(h))
+    for h in range(2):
         if count == OWNERS:
-            body()
+            drain(full.at[h, pl.ds(0, 120)], r3sem.at[h])
         else:
-            pl.when(me < OWNERS)(body)
-
-    if count == OWNERS:
-        peers(lambda t: to_owner(t).start())
-        drain(part.at[pl.ds(0, count - 1)], r2sem)
-    else:
-        for t in range(OWNERS):
-            pl.when(me != t)(lambda t=t: to_owner(t).start())
-        spread(lambda: drain(part.at[pl.ds(0, count - 1)], r2sem))
-
-    def publish():
-        at = pl.multiple_of(8 * me, 8)
-        part[me] = pack[pl.ds(at, 8)]
-        total = part[0]
-        if count <= 8:
-            for t in range(1, count):
-                total = total + part[t]
+            pl.when(me < OWNERS)(lambda: drain(full.at[h, pl.ds(0, 120)], r3sem.at[h]))
+            pl.when(me >= OWNERS)(lambda: drain(full.at[h], r3sem.at[h]))
+
+    result[...] = jnp.concatenate([full[0], full[1]], axis=1)
+
+    drain(gat.at[pl.ds(0, count - 1)], s1sem)
+    for h in range(2):
+        if count == OWNERS:
+            drain(part.at[h, pl.ds(0, count - 1)], s2sem.at[h])
         else:
-            total = lax.fori_loop(1, count, lambda t, acc: acc + part[t], total)
-        shard = full.at[pl.ds(pl.multiple_of(64 * core + 8 * me, 8), 8)]
-        shard[...] = total
-        remote(shard, shard, s3b, r3sem, me, other).start()
-        peers(lambda t: (remote(shard, shard, s3a, r3sem, t, core).start(),
-                         remote(shard, shard, s3b, r3sem, t, other).start()))
-
-    spread(publish)
-    if count == OWNERS:
-        drain(full.at[pl.ds(0, 120)], r3sem)
-    else:
-        pl.when(me < OWNERS)(lambda: drain(full.at[pl.ds(0, 120)], r3sem))
-        pl.when(me >= OWNERS)(lambda: drain(full, r3sem))
-
-    result[...] = full[...]
-
-    drain(gat.at[pl.ds(0, count - 1)], s1sem)
-    if count == OWNERS:
-        drain(part.at[pl.ds(0, count - 1)], s2sem)
-    else:
-        pl.when(me < OWNERS)(lambda: drain(pack.at[pl.ds(0, 56)], s2sem))
-        pl.when(me >= OWNERS)(lambda: drain(pack, s2sem))
-
-    def sent():
-        drain(part.at[pl.ds(0, count - 1)], s3a)
-        drain(part, s3b)
-
-    spread(sent)
+            pl.when(me < OWNERS)(lambda: drain(pack.at[h, pl.ds(0, 56)], s2sem.at[h]))
+            pl.when(me >= OWNERS)(lambda: drain(pack.at[h], s2sem.at[h]))
+
+    def sent(h):
+        drain(part.at[h, pl.ds(0, count - 1)], s3a.at[h])
+        drain(part.at[h], s3b.at[h])
+
+    for h in range(2):
+        spread(lambda: sent(h))
 
 
 GRADS = ((9, 3, 64), (1, 64), (9, 64, 64), (1, 64), (9, 2, 64), (1, 2))
@@ -462,10 +469,10 @@
             pltpu.VMEM((5, 4, 1024), f32),
             pltpu.VMEM((2, 5, 4, 1024), f32),
             pltpu.VMEM((count, 8, CW), f32),
-            pltpu.VMEM((64, 256), f32),
-            pltpu.VMEM((count, 8, 256), f32),
-            pltpu.VMEM((128, 256), f32),
-        ] + [dma] * 10 + [dma((6,))],
+            pltpu.VMEM((2, 64, 128), f32),
+            pltpu.VMEM((2, count, 8, 128), f32),
+            pltpu.VMEM((2, 128, 128), f32),
+        ] + [dma] * 4 + [dma((2,))] * 5 + [dma] + [dma((6,))],
         compiler_params=pltpu.CompilerParams(
             collective_id=0, has_side_effects=True, vmem_limit_bytes=62 * 1024 * 1024),
     )(initial, forcing, vx, vy, cot, w1.transpose(0, 2, 1), b1.reshape(1, 64), w2,

time: 27.2 us -> 27.4 us (level)
  no operation moved by 1% of the time
where the time goes in v4:
time: 27.4 us; the launch traced here: 27.2 us
  Pallas kernels  26.6 us (97%)
  between operations  0.64 us (2%)
    pallas_call x1, Pallas kernels, per_device(): pl.pallas_call(functools.partial(kernel, count), out_shape=jax.ShapeDtype...  24.8 us
    pallas_call x1, Pallas kernels, per_device(): pl.pallas_call(unpack, out_shape=[jax.ShapeDtypeStruct(s, f32) for s in G...  1.76 us

profile of v4, /device:TPU:0, one launch (start us, length us, event | category | flops | bytes accessed | tf_op | source)
XLA Modules:
  0.0 27.2 jit_solution(6463741410922759126)
XLA Ops:
  0.6 24.8 %shard_map.154.full = f32[128,256]{1,0:T(8,128)} custom-call(f32[4,1024]{1,0:T(4,128)} %initial.1, f32[1,4,1024]{2,1,0:T(4,128)} %forcing.1, f32[4,1024]{1,0:T(4,128)} %vel_x.1, f32[4,1024]{1,0:T(4,128)} %vel_y.1, f32[1,4,1024]{2,1,0:T(4,128)} %cot.1, f32[9,3,64]{2,1,0:T(4,128)} %bitcast.8, f32[1,64]{1,0:T(1,128)} %bitcast.9, f32[9,64,64]{2,1,0:T(8,128)} %middle_hbm.1, ...), custom_call_target="tpu_custom_call" | custom-call | tf_op jit(solution)/shard_map/pallas_call | solution.py:463
  25.5 1.8 %shard_map.155 = (f32[9,3,64]{2,1,0:T(4,128)}, f32[1,64]{1,0:T(1,128)}, f32[9,64,64]{2,1,0:T(8,128)}, f32[1,64]{1,0:T(1,128)}, f32[9,2,64]{2,1,0:T(2,128)}, /*index=5*/f32[1,2]{1,0:T(1,128)}) custom-call(f32[128,256]{1,0:T(8,128)} %shard_map.154.full), custom_call_target="tpu_custom_call" | custom-call | tf_op jit(solution)/shard_map/pallas_call | solution.py:480
